TPU v7x, 32 devices: a whole 2x2x4 slice. The times are simulated.
32 devices in a mesh: groups: 2 (over y), patch: 4 (over z), section: 2 (over x), head: 2 (over core).
Axes of the slice: x: 2, y: 2, z: 4, core: 2. Of those that a mesh axis runs over, the one named last changes fastest.
Arguments:
- ctrl_hidden: bfloat16 [2048, 3072], P(('groups', 'patch'), ('section', 'head')), parts along dimension 0, may hold values from -6 to 6
- base_hidden: bfloat16 [2048, 3072], P(('groups', 'patch'), ('section', 'head')), parts along dimension 0, may hold values from -6 to 6
- ctrl_qkv_weight: bfloat16 [3072, 3, 512], P('patch', None, ('section', 'head')), may hold values from -0.109375 to 0.109375
- base_qkv_weight: bfloat16 [3072, 3, 512], P('patch', None, ('section', 'head')), may hold values from -0.109375 to 0.109375
- ctrl_out_weight: bfloat16 [512, 3072], P(('section', 'head')), may hold values from -0.25 to 0.25
- base_out_weight: bfloat16 [512, 3072], P(('section', 'head')), may hold values from -0.25 to 0.25
- ctrl_mod: float32 [3, 3072], replicated, may hold values from -3 to 3
- base_mod: float32 [3, 3072], replicated, may hold values from -3 to 3
- ctrl_qk_gain: float32 [2, 128], replicated, may hold values from 0.7 to 24
- base_qk_gain: float32 [2, 128], replicated, may hold values from 0.7 to 24
- ctrl_stale: bfloat16 [2, 2048, 512], P(None, ('groups', 'patch'), ('section', 'head')), parts along dimension 1, may hold values from -6 to 6
- base_stale: bfloat16 [2, 2048, 512], P(None, ('groups', 'patch'), ('section', 'head')), parts along dimension 1, may hold values from -6 to 6
- ctrl_text: bfloat16 [2, 512, 512], P(None, 'groups', ('section', 'head')), parts along dimension 1, may hold values from -6 to 6
- base_text: bfloat16 [2, 512, 512], P(None, 'groups', ('section', 'head')), parts along dimension 1, may hold values from -6 to 6
- ctrl_order: int32 [16], replicated, may hold values from 0 to 15, as said below
- base_order: int32 [16], replicated, may hold values from 0 to 15, as said below
- text_len: int32 [2], P('groups'), parts along dimension 0, may hold values from 128 to 256
Outputs:
- ctrl_out: bfloat16 [2048, 3072], P(('groups', 'patch'), ('section', 'head')), parts along dimension 0
- base_out: bfloat16 [2048, 3072], P(('groups', 'patch'), ('section', 'head')), parts along dimension 0
There are 2 independent parts, one for each index of `groups`. A program takes and returns all parts, laid end to end along the dimension named above; an argument that names none is the same for every part. Nothing has to cross between parts.
Inputs may be any that keep to these rules, and one draw needn't show every extreme that they name: `ctrl_order`: a permutation of the 16 blocks. `base_order`: a permutation of the 16 blocks; each patch of the base layout holds exactly one block from each patch of the control layout.
All inputs are finite; a program needn't handle non-finite values.
Results may differ from a plain program's by a relative error of at most 0.012.
The roundings to bfloat16 on the way count: a program that leaves them out, or rounds other values in their place, can miss the bound.
Values may be sent and summed in bfloat16 or wider, within the bound.
A program may use at most 64 MiB of HBM per device.

v0:
```python
import jax
import jax.numpy as jnp
from jax import lax
from jax.sharding import PartitionSpec as P


def modulate(whole, mod):
    values = whole.astype(jnp.float32)
    center = jnp.mean(values, axis=-1, keepdims=True)
    spread = jnp.mean((values - center) ** 2, axis=-1, keepdims=True)
    normed = (values - center) * lax.rsqrt(spread + 1e-06)
    return (normed * (1.0 + mod[1]) + mod[0]).astype(jnp.bfloat16)


def rms_scale(values, gain):
    return values * lax.rsqrt(jnp.mean(values * values, axis=-1, keepdims=True) + 1e-06) * gain


def absorb_keys(carry, query, piece, own_start, own_rows):
    top, total, mixed = carry
    keys = piece[0]
    values = piece[1]
    rows = jnp.arange(keys.shape[0], dtype=jnp.int32)
    keep = (rows < own_start) | (rows >= own_start + own_rows)
    score = lax.dot_general(
        query, keys, (((1,), (1,)), ((), ())), preferred_element_type=jnp.float32
    )
    score = jnp.where(keep[None, :], score * query.shape[1] ** (-0.5), -1e30)
    fresh_top = jnp.maximum(top, jnp.max(score, axis=1))
    factor = jnp.exp(top - fresh_top)
    expo = jnp.exp(score - fresh_top[:, None])
    product = jnp.dot(expo.astype(jnp.bfloat16), values, preferred_element_type=jnp.float32)
    return (fresh_top, total * factor + jnp.sum(expo, axis=1), mixed * factor[:, None] + product)


def attend(hidden, qkv_weight, out_weight, mod, gain, stale, text, text_len):
    whole = lax.all_gather(hidden, ("section", "head"), axis=1, tiled=True)
    normed = modulate(whole, mod)
    tok_rows = hidden.shape[0]
    head_size = qkv_weight.shape[2]
    qkv = jnp.einsum(
        "tr,rcn->tcn",
        normed,
        lax.all_gather(qkv_weight, "patch", axis=0, tiled=True),
        preferred_element_type=jnp.float32,
    )
    query = rms_scale(qkv[:, 0], gain[0]).astype(jnp.bfloat16)
    key_new = rms_scale(qkv[:, 1], gain[1]).astype(jnp.bfloat16)
    value_new = qkv[:, 2].astype(jnp.bfloat16)
    text_slots = text.shape[1]
    keys = jnp.concatenate([text[0], key_new], axis=0)
    values = jnp.concatenate([text[1], value_new], axis=0)
    slots = jnp.arange(text_slots + tok_rows, dtype=jnp.int32)
    live = (slots < text_len[0]) | (slots >= text_slots)
    score = lax.dot_general(
        query, keys, (((1,), (1,)), ((), ())), preferred_element_type=jnp.float32
    )
    score = jnp.where(live[None, :], score * head_size ** (-0.5), -1e30)
    top = jnp.max(score, axis=1)
    expo = jnp.exp(score - top[:, None])
    carry = (
        top,
        jnp.sum(expo, axis=1),
        jnp.dot(expo.astype(jnp.bfloat16), values, preferred_element_type=jnp.float32),
    )
    own_start = lax.axis_index("patch") * tok_rows
    carry = absorb_keys(
        carry, query, lax.all_gather(stale, "patch", axis=1, tiled=True), own_start, tok_rows
    )
    attn = (carry[2] / carry[1][:, None]).astype(jnp.bfloat16)
    partial_rows = jnp.dot(attn, out_weight, preferred_element_type=jnp.float32)
    return lax.psum_scatter(
        partial_rows.astype(jnp.bfloat16), ("section", "head"), scatter_dimension=1, tiled=True
    ).astype(jnp.float32)


def inverse_of(order):
    count = order.shape[0]
    places = jnp.arange(count, dtype=jnp.int32)
    match = (order[None, :] == places[:, None]).astype(jnp.int32)
    return jnp.sum(match * places[None, :], axis=1)


def pick_small(table, index):
    places = jnp.arange(table.shape[0], dtype=jnp.int32)
    return jnp.sum((index[:, None] == places[None, :]).astype(jnp.int32) * table[None, :], axis=1)


def local(
    ctrl_hidden,
    base_hidden,
    ctrl_qkv_weight,
    base_qkv_weight,
    ctrl_out_weight,
    base_out_weight,
    ctrl_mod,
    base_mod,
    ctrl_qk_gain,
    base_qk_gain,
    ctrl_stale,
    base_stale,
    ctrl_text,
    base_text,
    ctrl_order,
    base_order,
    text_len,
):
    tok_rows, columns = ctrl_hidden.shape
    col_start = lax.axis_index(("section", "head")) * columns
    owners = lax.axis_size("patch")
    blocks_all = ctrl_order.shape[0]
    per_owner = blocks_all // owners
    blk_rows = tok_rows // per_owner
    ctrl_proj = attend(
        ctrl_hidden,
        ctrl_qkv_weight,
        ctrl_out_weight,
        ctrl_mod,
        ctrl_qk_gain,
        ctrl_stale,
        ctrl_text,
        text_len,
    )
    ctrl_gate = lax.dynamic_slice_in_dim(ctrl_mod[2], col_start, columns, 0)
    ctrl_out = (ctrl_hidden.astype(jnp.float32) + ctrl_gate * ctrl_proj).astype(jnp.bfloat16)
    patch_index = lax.axis_index("patch")
    ctrl_inverse = inverse_of(ctrl_order)
    my_base = lax.dynamic_slice_in_dim(base_order, patch_index * per_owner, per_owner, 0)
    source_pos = pick_small(ctrl_inverse, my_base)
    every_row = lax.all_gather(ctrl_out, "patch", axis=0, tiled=True)
    every_block = every_row.reshape(blocks_all, blk_rows, columns)
    select = (source_pos[:, None] == jnp.arange(blocks_all, dtype=jnp.int32)[None, :]).astype(
        jnp.bfloat16
    )
    relaid = jnp.einsum("jn,nbd->jbd", select, every_block, preferred_element_type=jnp.float32)
    relaid = relaid.reshape(tok_rows, columns)
    base_proj = attend(
        base_hidden,
        base_qkv_weight,
        base_out_weight,
        base_mod,
        base_qk_gain,
        base_stale,
        base_text,
        text_len,
    )
    base_gate = lax.dynamic_slice_in_dim(base_mod[2], col_start, columns, 0)
    base_out = (base_hidden.astype(jnp.float32) + base_gate * base_proj + relaid).astype(
        jnp.bfloat16
    )
    return (ctrl_out, base_out)


def solution(mesh):
    in_specs = (
        P(("groups", "patch"), ("section", "head")),
        P(("groups", "patch"), ("section", "head")),
        P("patch", None, ("section", "head")),
        P("patch", None, ("section", "head")),
        P(("section", "head"), None),
        P(("section", "head"), None),
        P(),
        P(),
        P(),
        P(),
        P(None, ("groups", "patch"), ("section", "head")),
        P(None, ("groups", "patch"), ("section", "head")),
        P(None, "groups", ("section", "head")),
        P(None, "groups", ("section", "head")),
        P(),
        P(),
        P("groups"),
    )
    out_specs = (
        P(("groups", "patch"), ("section", "head")),
        P(("groups", "patch"), ("section", "head")),
    )
    return jax.shard_map(local, mesh=mesh, in_specs=in_specs, out_specs=out_specs, check_vma=False)
```

profile of v0, /device:TPU:0, one launch (start us, length us, event | category | flops | bytes accessed | tf_op | source)
XLA Modules:
  0.0 263.3 jit_solution(7424464779098925015)
XLA Ops:
  7.2 0.7 all-gather.6.cloned.1.call-update
  8.0 0.7 all-gather.8.cloned.1.call-update
  8.7 0.7 all-gather.10.cloned.1.call-update
  10.7 1.0 fusion.103
  11.7 0.8 slice_bitcast_fusion.19
  12.4 0.9 slice_bitcast_fusion.14
  13.3 17.4 %all_gather.23 = bf16[2,1024,128]{2,1,0:T(8,128)(2,1)S(1)} all-gather(bf16[2,256,128]{2,1,0:T(8,128)(2,1)S(1)} %copy-done.8), channel_id=1, replica_groups=mesh['groups'=2,'patch'=4,'section'=2,'head'=2] {'patch'}, dimensions={1}, use_global_device_ids=true | all-gather | bytes 655360 | tf_op jit(solution)/shard_map/all_gather | solution.py:68
  30.7 1.3 all-gather.6.cloned.1.call-done
  32.0 1.8 convert_reduce_fusion.1
  33.9 0.6 fusion.8
  34.4 49.6 %all-gather.8.cloned.1.call-done = bf16[3072,3,128]{2,0,1:T(8,128)(2,1)} async-done(((bf16[768,3,128]{2,0,1:T(8,128)(2,1)}), bf16[3072,3,128]{2,0,1:T(8,128)(2,1)}) %all-gather.8.cloned.1.call-update) | async-done | bytes 2359312 | tf_op jit(solution)/shard_map/all_gather | solution.py:44
  84.0 2.7 %fusion.13 = f32[256,3,128]{2,0,1:T(8,128)S(1)} fusion(bf16[3072,3,128]{2,0,1:T(8,128)(2,1)} %all-gather.8.cloned.1.call-done, bf16[256,3072]{1,0:T(8,128)(2,1)S(1)} %copy-done.2, f32[3072]{0:T(1024)S(1)} %bitcast.109, f32[3072]{0:T(1024)S(1)} %bitcast.110, f32[256]{0:T(256)S(1)} %add_rsqrt_fusion.5, f32[256]{0:T(256)S(1)} %broadcast_multiply_fusion.1), kind=kOutput, calls=%fused_computation.19 | convolution fusion | flops 608698368 | bytes 4352000 | tf_op jit(solution)/shard_map/tr,rcn->tcn/dot_general | solution.py:41
  88.8 2.0 convolution_convert_fusion.1
  90.9 16.0 %all_gather.26 = bf16[2,1024,128]{2,1,0:T(8,128)(2,1)S(1)} all-gather(bf16[2,256,128]{2,1,0:T(8,128)(2,1)S(1)} %copy-done.9), channel_id=1, replica_groups=mesh['groups'=2,'patch'=4,'section'=2,'head'=2] {'patch'}, dimensions={1}, use_global_device_ids=true | all-gather | bytes 655360 | tf_op jit(solution)/shard_map/all_gather | solution.py:68
  106.9 0.6 slice_bitcast_fusion.12
  107.6 1.8 convert_reduce_fusion
  109.5 0.6 fusion.4
  110.0 46.0 %all-gather.12.cloned.1.call-done = bf16[3072,3,128]{2,0,1:T(8,128)(2,1)} async-done(((bf16[768,3,128]{2,0,1:T(8,128)(2,1)}), bf16[3072,3,128]{2,0,1:T(8,128)(2,1)}) %all-gather.12.cloned.1.call-update) | async-done | bytes 2359312 | tf_op jit(solution)/shard_map/all_gather | solution.py:44
  156.0 2.8 %fusion.16 = f32[256,3,128]{2,0,1:T(8,128)S(1)} fusion(bf16[3072,3,128]{2,0,1:T(8,128)(2,1)} %all-gather.12.cloned.1.call-done, bf16[256,3072]{1,0:T(8,128)(2,1)S(1)} %copy-done.1, f32[3072]{0:T(1024)S(1)} %bitcast.111, f32[3072]{0:T(1024)S(1)} %bitcast.112, f32[256]{0:T(256)S(1)} %add_rsqrt_fusion.2, f32[256]{0:T(256)S(1)} %broadcast_multiply_fusion), kind=kOutput, calls=%fused_computation.21 | convolution fusion | flops 608698368 | bytes 4352000 | tf_op jit(solution)/shard_map/tr,rcn->tcn/dot_general | solution.py:41
  158.8 0.7 copy-done.5
  159.7 25.8 %reduce-scatter.3.cloned.1.call-done = bf16[256,768]{1,0:T(8,128)(2,1)} async-done(((bf16[256,3072]{1,0:T(8,128)(2,1)}), bf16[256,768]{1,0:T(8,128)(2,1)}) %reduce-scatter.3.cloned.1.call-update) | async-done | bytes 393232 | tf_op jit(solution)/shard_map/reduce_scatter | solution.py:72
  185.5 1.9 add_convert_fusion
  187.5 1.0 multiply_convert_fusion.1
  188.5 1.3 fusion.106
  189.8 1.0 fusion.107
  191.4 0.6 multiply_add_fusion
  192.0 1.1 convolution_multiply_fusion.4
  193.2 2.7 %convolution_convert_fusion = bf16[256,3072]{1,0:T(8,128)(2,1)} fusion(bf16[128,3072]{1,0:T(8,128)(2,1)S(1)} %copy-done.7, f32[256,128]{1,0:T(8,128)S(1)} %convolution_multiply_fusion.4, f32[256,1024]{1,0:T(8,128)S(1)} %get-tuple-element.31, f32[256]{0:T(256)S(1)} %max.27, bf16[2,1024,128]{2,1,0:T(8,128)(2,1)S(1)} %all_gather.26, f32[256]{0:T(256)} %get-tuple-element.6), kind=kOutput, calls=%fused_computation.4 | convolution fusion | flops 269844480 | bytes 3803136 | tf_op jit(solution)/shard_map/dot_general | solution.py:71
  196.3 28.4 %all-gather.14.cloned.1.call-done = bf16[1024,768]{1,0:T(8,128)(2,1)} async-done(((bf16[256,768]{1,0:T(8,128)(2,1)}), bf16[1024,768]{1,0:T(8,128)(2,1)}) %all-gather.14.cloned.1.call-update) | async-done | bytes 1572880 | tf_op jit(solution)/shard_map/all_gather | solution.py:130
  224.7 2.4 fusion.18
  227.3 27.2 %reduce-scatter.5.cloned.1.call-done = bf16[256,768]{1,0:T(8,128)(2,1)} async-done(((bf16[256,3072]{1,0:T(8,128)(2,1)}), bf16[256,768]{1,0:T(8,128)(2,1)}) %reduce-scatter.5.cloned.1.call-update) | async-done | bytes 393232 | tf_op jit(solution)/shard_map/reduce_scatter | solution.py:72
  254.5 1.9 fusion.40
  (76 shorter events, 4.3 us)
Async XLA Ops:
  7.2 81.5 %copy-start = (bf16[128,3072]{1,0:T(8,128)(2,1)S(1)}, bf16[128,3072]{1,0:T(8,128)(2,1)}, u32[]{:S(2)}) copy-start(bf16[128,3072]{1,0:T(8,128)(2,1)} %param.21) | copy-start | bytes 2359300
  7.2 6.1 %copy-start.8 = (bf16[2,256,128]{2,1,0:T(8,128)(2,1)S(1)}, bf16[2,256,128]{2,1,0:T(8,128)(2,1)}, u32[]{:S(2)}) copy-start(bf16[2,256,128]{2,1,0:T(8,128)(2,1)} %param.27) | copy-start | bytes 393220
  7.2 24.8 %all-gather.6.cloned.1.call-start = ((), (), s32[]{:S(2)}) async-start(), calls=%async_computation.2 | async-start | bytes 1966080 | tf_op jit(solution)/shard_map/all_gather | solution.py:37
  7.9 76.1 %all-gather.8.cloned.1.call-start = ((), (), s32[]{:S(2)}) async-start(), calls=%async_computation.3 | async-start | bytes 2949120 | tf_op jit(solution)/shard_map/all_gather | solution.py:44
  8.7 98.9 %all-gather.10.cloned.1.call-start = ((), (), s32[]{:S(2)}) async-start(), calls=%async_computation.5 | async-start | bytes 1966080 | tf_op jit(solution)/shard_map/all_gather | solution.py:37
  9.4 146.6 %all-gather.12.cloned.1.call-start = ((), (), s32[]{:S(2)}) async-start(), calls=%async_computation.6 | async-start | bytes 2949120 | tf_op jit(solution)/shard_map/all_gather | solution.py:44
  10.0 175.5 %reduce-scatter.3.cloned.1.call-start = ((), (), s32[]{:S(2)}) async-start(), calls=%async_computation.4 | async-start | bytes 1966080 | tf_op jit(solution)/shard_map/reduce_scatter | solution.py:72
  32.0 1.9 copy-start.2
  88.7 2.2 copy-start.9
  88.7 18.2 %copy-start.13 = (f32[2,128]{1,0:T(2,128)S(1)}, f32[2,128]{1,0:T(2,128)}, u32[]{:S(2)}) copy-start(f32[2,128]{1,0:T(2,128)} %param.26) | copy-start | bytes 3076
  88.7 18.2 %copy-start.10 = (bf16[2,256,128]{2,1,0:T(8,128)(2,1)S(1)}, bf16[2,256,128]{2,1,0:T(8,128)(2,1)}, u32[]{:S(2)}) copy-start(bf16[2,256,128]{2,1,0:T(8,128)(2,1)} %param.30) | copy-start | bytes 393220
  88.7 18.8 %copy-start.11 = (f32[3,3072]{1,0:T(4,128)S(1)}, f32[3,3072]{1,0:T(4,128)}, u32[]{:S(2)}) copy-start(f32[3,3072]{1,0:T(4,128)} %param.24) | copy-start | bytes 110596
  90.8 133.9 %all-gather.14.cloned.1.call-start = ((), (), s32[]{:S(2)}) async-start(), calls=%async_computation.8 | async-start | bytes 1966080 | tf_op jit(solution)/shard_map/all_gather | solution.py:130
  106.9 81.6 %copy-start.12 = (f32[128]{0:T(128)}, f32[128]{0:T(128)S(1)}, u32[]{:S(2)}) copy-start(f32[128]{0:T(128)S(1)} %get-tuple-element.20) | copy-start | bytes 1540
  107.6 1.9 copy-start.1
  156.0 29.4 %copy-start.3 = (bf16[256,768]{1,0:T(8,128)(2,1)S(1)}, bf16[256,768]{1,0:T(8,128)(2,1)}, u32[]{:S(2)}) copy-start(bf16[256,768]{1,0:T(8,128)(2,1)} %param.17) | copy-start | bytes 1179652
  158.8 0.7 copy-start.5
  159.7 30.1 %copy-start.6 = (f32[256,3,128]{2,0,1:T(8,128)S(1)}, f32[256,3,128]{2,0,1:T(8,128)}, u32[]{:S(2)}) copy-start(f32[256,3,128]{2,0,1:T(8,128)} %copy-done.5) | copy-start | bytes 1179652
  187.4 67.1 %reduce-scatter.5.cloned.1.call-start = ((), (), s32[]{:S(2)}) async-start(), calls=%async_computation.7 | async-start | bytes 1966080 | tf_op jit(solution)/shard_map/reduce_scatter | solution.py:72
  188.5 4.7 %copy-start.7 = (bf16[128,3072]{1,0:T(8,128)(2,1)S(1)}, bf16[128,3072]{1,0:T(8,128)(2,1)}, u32[]{:S(2)}) copy-start(bf16[128,3072]{1,0:T(8,128)(2,1)} %param.22) | copy-start | bytes 2359300
  193.1 2.8 %copy-start.14 = (s32[16]{0:T(128)S(1)}, s32[16]{0:T(128)}, u32[]{:S(2)}) copy-start(s32[16]{0:T(128)} %param.32) | copy-start | bytes 196
  193.1 2.9 %copy-start.15 = (s32[16]{0:T(128)S(1)}, s32[16]{0:T(128)}, u32[]{:S(2)}) copy-start(s32[16]{0:T(128)} %param.31) | copy-start | bytes 196
  195.9 58.6 %copy-start.4 = (bf16[256,768]{1,0:T(8,128)(2,1)S(1)}, bf16[256,768]{1,0:T(8,128)(2,1)}, u32[]{:S(2)}) copy-start(bf16[256,768]{1,0:T(8,128)(2,1)} %param.18) | copy-start | bytes 1179652
Sparse Core Ops, SparseCore 0:
  9.6 22.3 all-gather.5
  33.5 50.4 all-gather.7
  85.6 18.4 all-gather.9
  105.6 50.4 all-gather.11
  158.4 27.0 reduce-scatter.2
  187.6 37.1 all-gather.13
  227.4 27.0 reduce-scatter.4
where the time goes:
time: 264 us; the launch traced here: 263 us
  waiting for transfers between devices  181 us (69%)
  blocking collectives  33.3 us (13%)
  matrix products  17.2 us (7%)
  between operations  15.1 us (6%)
  other arithmetic  12.9 us (5%)
  local copies, waits for them, and re-layouts  3.48 us (1%)
    all_gather x2, waiting for transfers between devices, attend(): lax.all_gather(qkv_weight, 'patch', axis=0, tiled=True)  95.6 us
    reduce_scatter x2, waiting for transfers between devices, attend(): lax.psum_scatter(partial_rows.astype(jnp.bfloat16), ('section', 'head'),...  52.9 us
    all_gather x2, blocking collectives, attend(): lax.all_gather(stale, 'patch', axis=1, tiled=True)  33.3 us
    all_gather x1, waiting for transfers between devices, local(): every_row = lax.all_gather(ctrl_out, 'patch', axis=0, tiled=True)  28.4 us
    dot_general x2, matrix products, attend(): jnp.einsum('tr,rcn->tcn', normed, lax.all_gather(qkv_weight, 'patch', axi...  5.5 us
  transfers between devices with their start and end apart: 7, of which 6 were waited for; matrix products, arithmetic and copies ran while one was open for 11% of the time, Pallas kernels for 0%

commit v1 on v0

v1 whole, which is shorter than its diff:
```python
import functools

import jax
import jax.numpy as jnp
from jax import lax
from jax.experimental import pallas as pl
from jax.experimental.pallas import tpu as pltpu
from jax.sharding import PartitionSpec as P

F32 = jnp.float32
BF16 = jnp.bfloat16


def kernel(
    sizes,
    text_len,
    ctrl_order,
    base_order,
    hid0,
    hid1,
    w0,
    w1,
    wo0,
    wo1,
    mod0,
    mod1,
    gain0,
    gain1,
    stale0,
    stale1,
    text0,
    text1,
    out0,
    out1,
    hbuf,
    wbuf,
    kvbuf,
    psend,
    pbuf,
    hn,
    score_buf,
    blk_send,
    blk_buf,
    h_send,
    h_fwd,
    h_recv,
    w_send,
    w_recv,
    y_send,
    y_recv,
    kv_send,
    kv_recv,
    p_send,
    p_recv,
    b_send,
    b_recv,
):
    n_groups, n_patch, n_sec, n_head = sizes
    n_sh = n_sec * n_head
    hids, ws, wos = (hid0, hid1), (w0, w1), (wo0, wo1)
    mods, gains, stales, texts, outs = (
        (mod0, mod1),
        (gain0, gain1),
        (stale0, stale1),
        (text0, text1),
        (out0, out1),
    )
    rows, cols = hid0.shape
    head_size = stale0.shape[2]
    width = n_sh * cols
    blk = rows // n_patch
    g = lax.axis_index("groups")
    z = lax.axis_index("patch")
    x = lax.axis_index("section")
    c = lax.axis_index("head")
    me = x * n_head + c
    other = 1 - c

    def device(g_=None, z_=None, x_=None, c_=None):
        return (
            g if g_ is None else g_,
            z if z_ is None else z_,
            x if x_ is None else x_,
            c if c_ is None else c_,
        )

    def remote(src, dst, send, recv, dev):
        return pltpu.make_async_remote_copy(
            src_ref=src,
            dst_ref=dst,
            send_sem=send,
            recv_sem=recv,
            device_id=dev,
            device_id_type=pl.DeviceIdType.MESH,
        )

    def hid_copy(b, k):
        src = hids[b]
        if k == 0:
            dev = device(c_=other)
        else:
            dev = device(x_=lax.rem(x + k, n_sec))
        return remote(src, hbuf.at[b, me], h_send.at[b, k], h_recv.at[b, me], dev)

    def hid_start(b):
        for k in list(range(1, n_sec)) + [0]:
            hid_copy(b, k).start()
        hbuf[b, me] = hids[b][...]

    def hid_fwd_copy(b, k):
        j = lax.rem(x + n_sec - k, n_sec) * n_head + c
        return remote(
            hbuf.at[b, j], hbuf.at[b, j], h_fwd.at[b, k], h_recv.at[b, j], device(c_=other)
        )

    def hid_forward(b):
        for k in range(1, n_sec):
            copy = hid_fwd_copy(b, k)
            copy.wait_recv()
            copy.start()

    def hid_wait(b):
        for k in range(n_sec):
            j = lax.rem(x + n_sec - k, n_sec) * n_head + other
            remote(
                hbuf.at[b, j], hbuf.at[b, j], h_fwd.at[b, 0], h_recv.at[b, j], device(c_=other)
            ).wait_recv()

    def w_copy(b, t, side):
        j = z - t if side == 0 else z + t
        src = ws[b].at[g] if t == 0 else wbuf.at[b, j, g]
        dev = device(z_=z + 1 if side == 0 else z - 1)
        return remote(src, wbuf.at[b, j, g], w_send.at[b, side, t], w_recv.at[b, j], dev)

    def kv_copy(b, t, side):
        j = z - t if side == 0 else z + t
        src = stales[b] if t == 0 else kvbuf.at[b, j]
        dev = device(z_=z + 1 if side == 0 else z - 1)
        return remote(src, kvbuf.at[b, j], kv_send.at[b, side, t], kv_recv.at[b, j], dev)

    def sends(t, side):
        if side == 0:
            return (z - t >= 0) & (z + 1 < n_patch)
        return (z + t < n_patch) & (z - 1 >= 0)

    def receives(t, side):
        return z - t - 1 >= 0 if side == 0 else z + t + 1 < n_patch

    def y_copy(b, j):
        return remote(
            wbuf.at[b, j, g], wbuf.at[b, j, g], y_send.at[b, j], y_recv.at[b, j], device(g_=1 - g)
        )

    def chain_start(make, b, t):
        for side in range(2):

            @pl.when(sends(t, side))
            def _():
                make(b, t, side).start()

    def w_arrive(b, t):
        for side in range(2):

            @pl.when(receives(t, side))
            def _():
                j = z - t - 1 if side == 0 else z + t + 1
                copy = remote(
                    wbuf.at[b, j, g],
                    wbuf.at[b, j, g],
                    y_send.at[b, j],
                    w_recv.at[b, j],
                    device(g_=1 - g),
                )
                copy.wait_recv()

        if t + 1 < n_patch - 1:
            chain_start(w_copy, b, t + 1)
        for side in range(2):

            @pl.when(receives(t, side))
            def _():
                y_copy(b, z - t - 1 if side == 0 else z + t + 1).start()

    def kv_arrive(b, t):
        for side in range(2):

            @pl.when(receives(t, side))
            def _():
                j = z - t - 1 if side == 0 else z + t + 1
                remote(
                    kvbuf.at[b, j],
                    kvbuf.at[b, j],
                    kv_send.at[b, side, 0],
                    kv_recv.at[b, j],
                    device(g_=1 - g),
                ).wait_recv()

        if t + 1 < n_patch - 1:
            chain_start(kv_copy, b, t + 1)

    def w_wait(b):
        for k in range(1, n_patch):
            j = lax.rem(z + k, n_patch)
            remote(
                wbuf.at[b, j, 1 - g],
                wbuf.at[b, j, 1 - g],
                y_send.at[b, j],
                y_recv.at[b, j],
                device(g_=1 - g),
            ).wait_recv()

    def normalize(b):
        step = min(32, rows)
        mod = mods[b]

        def body(i, carry):
            at = pl.ds(pl.multiple_of(i * step, step), step)
            total = jnp.zeros((step, 1), F32)
            for s in range(n_sh):
                total += jnp.sum(hbuf[b, s, at, :].astype(F32), axis=1, keepdims=True)
            center = total * (1.0 / width)
            spread = jnp.zeros((step, 1), F32)
            for s in range(n_sh):
                diff = hbuf[b, s, at, :].astype(F32) - center
                spread += jnp.sum(diff * diff, axis=1, keepdims=True)
            inv = lax.rsqrt(spread * (1.0 / width) + 1e-06)
            for s in range(n_sh):
                normed = (hbuf[b, s, at, :].astype(F32) - center) * inv
                hn[s, at, :] = (normed * (1.0 + mod[n_sh + s]) + mod[s]).astype(BF16)
            return carry

        lax.fori_loop(0, rows // step, body, 0)

    def rms(values, gain):
        mean = jnp.mean(values * values, axis=-1, keepdims=True)
        return (values * lax.rsqrt(mean + 1e-06) * gain).astype(BF16)

    def project(b):
        half = ws[b].shape[1]

        def body(s, acc):
            for part in range(2):
                acc += jnp.dot(
                    hn[s, :, part * half : (part + 1) * half],
                    wbuf[b, s, part],
                    preferred_element_type=F32,
                )
            return acc

        qkv = lax.fori_loop(0, n_sh, body, jnp.zeros((rows, 3 * head_size), F32))
        gain = gains[b]
        query = rms(qkv[:, :head_size], gain[0:1, :])
        kvbuf[b, z, 0] = rms(qkv[:, head_size : 2 * head_size], gain[1:2, :])
        kvbuf[b, z, 1] = qkv[:, 2 * head_size :].astype(BF16)
        return query

    def attend(b, query):
        scale = head_size ** (-0.5)
        text = texts[b]

        def scores(keys):
            return (
                lax.dot_general(query, keys, (((1,), (1,)), ((), ())), preferred_element_type=F32)
                * scale
            )

        slots = text.shape[1]
        text_score = scores(text[0])
        spot = lax.broadcasted_iota(jnp.int32, (rows, slots), 1)
        text_score = jnp.where(spot < text_len[0], text_score, -1e30)
        top = jnp.max(text_score, axis=1, keepdims=True)

        def first(s, top):
            score = scores(kvbuf[b, s, 0])
            score_buf[s] = score
            return jnp.maximum(top, jnp.max(score, axis=1, keepdims=True))

        top = lax.fori_loop(0, n_patch, first, top)
        expo = jnp.exp(text_score - top)
        total = jnp.sum(expo, axis=1, keepdims=True)
        mixed = jnp.dot(expo.astype(BF16), text[1], preferred_element_type=F32)

        def second(s, carry):
            total, mixed = carry
            expo = jnp.exp(score_buf[s] - top)
            return (
                total + jnp.sum(expo, axis=1, keepdims=True),
                mixed + jnp.dot(expo.astype(BF16), kvbuf[b, s, 1], preferred_element_type=F32),
            )

        total, mixed = lax.fori_loop(0, n_patch, second, (total, mixed))
        return (mixed / total).astype(BF16)

    def p_copy(b, k):
        s = peer(k)
        return remote(
            psend.at[b, s],
            pbuf.at[b, me],
            p_send.at[b, s],
            p_recv.at[b, me],
            device(x_=s // n_head, c_=lax.rem(s, n_head)),
        )

    def peer(k):
        if k < n_sh - n_head:
            return lax.rem(x + 1 + k // n_head, n_sec) * n_head + lax.rem(c + k, n_head)
        return x * n_head + (other if k == n_sh - n_head else c)

    def out_part(b, attn, s):
        wo = wos[b]
        if len(wo.shape) == 3:
            weight = wo[s]
        else:
            weight = wo[:, pl.ds(pl.multiple_of(s * cols, cols), cols)]
        return jnp.dot(attn, weight, preferred_element_type=F32).astype(BF16)

    def out_start(b, attn):
        for k in range(n_sh - 1):
            s = peer(k)
            psend[b, s] = out_part(b, attn, s)
            p_copy(b, k).start()
        pbuf[b, me] = out_part(b, attn, me)

    def out_wait(b):
        for k in range(n_sh - 1):
            s = peer(k)
            remote(
                psend.at[b, s], pbuf.at[b, s], p_send.at[b, s], p_recv.at[b, s], device(c_=other)
            ).wait_recv()

    def gated(b, at):
        total = pbuf[b, 0, at, :].astype(F32)
        for s in range(1, n_sh):
            total += pbuf[b, s, at, :].astype(F32)
        return hids[b][at, :].astype(F32) + mods[b][2 * n_sh + me] * total

    def ctrl_finish():
        for d in range(n_patch):
            at = pl.ds(d * blk, blk)
            out0[at, :] = gated(0, at).astype(BF16)

    def b_copy(k):
        d = lax.rem(z + k, n_patch)
        return remote(blk_send.at[d], blk_buf.at[z], b_send.at[d], b_recv.at[z], device(z_=d))

    def equal(one, two):
        return (one == two).astype(F32)

    def relay_start():
        def block_for(d):
            def outer(j, block):
                def inner(i, found):
                    return found + equal(base_order[d * n_patch + i], ctrl_order[z * n_patch + j])

                found = lax.fori_loop(0, n_patch, inner, jnp.float32(0.0))
                at = pl.ds(pl.multiple_of(j * blk, blk), blk)
                return block + found * out0[at, :].astype(F32)

            return lax.fori_loop(0, n_patch, outer, jnp.zeros((blk, cols), F32)).astype(BF16)

        for k in range(1, n_patch):
            d = lax.rem(z + k, n_patch)
            blk_send[d] = block_for(d)
            b_copy(k).start()
        blk_buf[z] = block_for(z)

    def relay_wait():
        for k in range(1, n_patch):
            d = lax.rem(z + k, n_patch)
            remote(
                blk_send.at[d], blk_buf.at[d], b_send.at[d], b_recv.at[d], device(z_=d)
            ).wait_recv()

    def base_finish():
        for i in range(n_patch):
            at = pl.ds(i * blk, blk)

            def outer(s, block):
                def inner(j, found):
                    return found + equal(ctrl_order[s * n_patch + j], base_order[z * n_patch + i])

                found = lax.fori_loop(0, n_patch, inner, jnp.float32(0.0))
                return block + found * blk_buf[s].astype(F32)

            relaid = lax.fori_loop(0, n_patch, outer, jnp.zeros((blk, cols), F32))
            out1[at, :] = (gated(1, at) + relaid).astype(BF16)

    barrier = pltpu.get_barrier_semaphore()
    partners = [device(g_=1 - g)]
    partners += [device(z_=lax.rem(z + k, n_patch)) for k in range(1, n_patch)]
    for k in range(n_sh - 1):
        s = peer(k)
        partners.append(device(x_=s // n_head, c_=lax.rem(s, n_head)))
    for partner in partners:
        pl.semaphore_signal(
            barrier, inc=1, device_id=partner, device_id_type=pl.DeviceIdType.MESH
        )
    pl.semaphore_wait(barrier, len(partners))

    last = n_patch - 1
    chain_start(w_copy, 0, 0)
    hid_start(0)
    chain_start(kv_copy, 0, 0)
    wbuf[0, z] = ws[0][...]
    wbuf[1, z] = ws[1][...]
    hid_start(1)
    hid_forward(0)
    w_arrive(0, 0)
    kv_arrive(0, 0)
    chain_start(w_copy, 1, 0)
    for t in range(1, last):
        w_arrive(0, t)
        kv_arrive(0, t)
        if t == 1:
            hid_wait(0)
            normalize(0)
            hid_forward(1)
            chain_start(kv_copy, 1, 0)
    w_arrive(1, 0)
    w_wait(0)
    query = project(0)
    kv_arrive(1, 0)
    for t in range(1, last - 1):
        w_arrive(1, t)
        kv_arrive(1, t)
    out_start(0, attend(0, query))
    w_arrive(1, last - 1)
    kv_arrive(1, last - 1)
    hid_wait(1)
    normalize(1)
    out_wait(0)
    ctrl_finish()
    relay_start()
    w_wait(1)
    query = project(1)
    out_start(1, attend(1, query))
    relay_wait()
    out_wait(1)
    base_finish()

    for b in range(2):
        for k in range(n_sec):
            hid_copy(b, k).wait_send()
        for k in range(1, n_sec):
            hid_fwd_copy(b, k).wait_send()
        for t in range(last):
            for side in range(2):

                @pl.when(sends(t, side))
                def _():
                    w_copy(b, t, side).wait_send()
                    kv_copy(b, t, side).wait_send()

        for k in range(1, n_patch):
            y_copy(b, lax.rem(z + k, n_patch)).wait_send()
        for k in range(n_sh - 1):
            p_copy(b, k).wait_send()
    for k in range(1, n_patch):
        b_copy(k).wait_send()


def local(
    sizes,
    ctrl_hidden,
    base_hidden,
    ctrl_qkv_weight,
    base_qkv_weight,
    ctrl_out_weight,
    base_out_weight,
    ctrl_mod,
    base_mod,
    ctrl_qk_gain,
    base_qk_gain,
    ctrl_stale,
    base_stale,
    ctrl_text,
    base_text,
    ctrl_order,
    base_order,
    text_len,
):
    n_groups, n_patch, n_sec, n_head = sizes
    n_sh = n_sec * n_head
    rows, cols = ctrl_hidden.shape
    w_rows, _, head_size = ctrl_qkv_weight.shape
    blk = rows // n_patch

    def halves(weight):
        return weight.reshape(2, w_rows // 2, 3 * head_size)

    def by_columns(weight):
        if cols % 128 == 0:
            return weight
        return weight.reshape(weight.shape[0], n_sh, cols).transpose(1, 0, 2)

    def mod_rows(mod):
        return mod.reshape(3 * n_sh, 1, cols)

    smem = pl.BlockSpec(memory_space=pltpu.SMEM)
    vmem = pl.BlockSpec(memory_space=pltpu.VMEM)
    dma = pltpu.SemaphoreType.DMA
    out = jax.ShapeDtypeStruct((rows, cols), BF16)
    return pl.pallas_call(
        functools.partial(kernel, sizes),
        out_shape=(out, out),
        in_specs=[smem] * 3 + [vmem] * 14,
        out_specs=(vmem, vmem),
        scratch_shapes=[
            pltpu.VMEM((2, n_sh, rows, cols), BF16),
            pltpu.VMEM((2, n_patch, 2, w_rows // 2, 3 * head_size), BF16),
            pltpu.VMEM((2, n_patch, 2, rows, head_size), BF16),
            pltpu.VMEM((2, n_sh, rows, cols), BF16),
            pltpu.VMEM((2, n_sh, rows, cols), BF16),
            pltpu.VMEM((n_sh, rows, cols), BF16),
            pltpu.VMEM((n_patch, rows, rows), F32),
            pltpu.VMEM((n_patch, blk, cols), BF16),
            pltpu.VMEM((n_patch, blk, cols), BF16),
            dma((2, n_sec)),
            dma((2, n_sec)),
            dma((2, n_sh)),
            dma((2, 2, n_patch)),
            dma((2, n_patch)),
            dma((2, n_patch)),
            dma((2, n_patch)),
            dma((2, 2, n_patch)),
            dma((2, n_patch)),
            dma((2, n_sh)),
            dma((2, n_sh)),
            dma((n_patch,)),
            dma((n_patch,)),
        ],
        compiler_params=pltpu.CompilerParams(
            collective_id=0, has_side_effects=True, vmem_limit_bytes=52 * 1024 * 1024
        ),
    )(
        text_len,
        ctrl_order,
        base_order,
        ctrl_hidden,
        base_hidden,
        halves(ctrl_qkv_weight),
        halves(base_qkv_weight),
        by_columns(ctrl_out_weight),
        by_columns(base_out_weight),
        mod_rows(ctrl_mod),
        mod_rows(base_mod),
        ctrl_qk_gain,
        base_qk_gain,
        ctrl_stale,
        base_stale,
        ctrl_text,
        base_text,
    )


def solution(mesh):
    sizes = tuple(mesh.shape[name] for name in ("groups", "patch", "section", "head"))
    in_specs = (
        P(("groups", "patch"), ("section", "head")),
        P(("groups", "patch"), ("section", "head")),
        P("patch", None, ("section", "head")),
        P("patch", None, ("section", "head")),
        P(("section", "head"), None),
        P(("section", "head"), None),
        P(),
        P(),
        P(),
        P(),
        P(None, ("groups", "patch"), ("section", "head")),
        P(None, ("groups", "patch"), ("section", "head")),
        P(None, "groups", ("section", "head")),
        P(None, "groups", ("section", "head")),
        P(),
        P(),
        P("groups"),
    )
    out_specs = (
        P(("groups", "patch"), ("section", "head")),
        P(("groups", "patch"), ("section", "head")),
    )
    return jax.shard_map(
        functools.partial(local, sizes),
        mesh=mesh,
        in_specs=in_specs,
        out_specs=out_specs,
        check_vma=False,
    )
```

time: 264 us -> 106 us (0.40)
  waiting for transfers between devices: 181 us -> 0 us
  Pallas kernels: 0 us -> 96.8 us
  blocking collectives: 33.3 us -> 0 us
  matrix products: 17.2 us -> 0 us
  between operations: 15.1 us -> 1.46 us
  other arithmetic: 12.9 us -> 0 us
  local copies, waits for them, and re-layouts: 3.48 us -> 7.06 us
    all_gather x5 -> x0, waiting for transfers between devices: 125 us -> none  [the longest x2 95.6 us: attend(): lax.all_gather(qkv_weight, 'patch', axis=0, tiled=True)]
    pallas_call x0 -> x1, Pallas kernels: none -> 96.8 us  [local(): pl.pallas_call(functools.partial(kernel, sizes), out_shape=(out, out), in...]
    reduce_scatter x2 -> x0, waiting for transfers between devices: 52.9 us -> none  [attend(): lax.psum_scatter(partial_rows.astype(jnp.bfloat16), ('section', 'head'),...]
    all_gather x2 -> x0, blocking collectives: 33.3 us -> none  [attend(): lax.all_gather(stale, 'patch', axis=1, tiled=True)]
    dot_general x11 -> x0, matrix products: 17.2 us -> none  [the longest x2 5.5 us: attend(): jnp.einsum('tr,rcn->tcn', normed, lax.all_gather(qkv_weight, 'patch', axi...]
    reduce_sum x12 -> x0, other arithmetic: 6.39 us -> none  [the longest x2 3.63 us: modulate(): center = jnp.mean(values, axis=-1, keepdims=True)]
    reshape x0 -> x6, local copies, waits for them, and re-layouts: none -> 5.5 us  [the longest x4 4.59 us: halves(): return weight.reshape(2, w_rows // 2, 3 * head_size)]
    convert_element_type x4 -> x0, other arithmetic: 4.9 us -> none  [the longest x1 1.93 us: local(): (base_hidden.astype(jnp.float32) + base_gate * base_proj + relaid).astype...]
  transfers between devices with their start and end apart: 7 -> 0, of which waited for: 6 -> 0; matrix products, arithmetic and copies ran while one was open for 11% -> 0% of each run, Pallas kernels for 0% -> 0%
where the time goes in v1:
time: 106 us; the launch traced here: 105 us
  Pallas kernels  96.8 us (91%)
  local copies, waits for them, and re-layouts  7.06 us (7%)
  between operations  1.46 us (1%)
    pallas_call x1, Pallas kernels, local(): pl.pallas_call(functools.partial(kernel, sizes), out_shape=(out, out), in...  96.8 us
    reshape x4, local copies, waits for them, and re-layouts, halves(): return weight.reshape(2, w_rows // 2, 3 * head_size)  4.59 us

profile of v1, /device:TPU:0, one launch (start us, length us, event | category | flops | bytes accessed | tf_op | source)
XLA Modules:
  0.0 105.3 jit_solution(13688036300047965876)
XLA Ops:
  0.6 0.0 copy-start.10
  1.3 0.9 reshape.18.mod0
  2.1 0.0 copy-done.10
  2.2 0.1 reshape.19.mod1
  2.2 1.6 %copy.25 = bf16[768,3,128]{2,1,0:T(4,128)(2,1)S(1)} copy(bf16[768,3,128]{2,0,1:T(8,128)(2,1)} %param.19) | data formatting | bytes 1179648 | tf_op jit(solution)/shard_map/reshape | solution.py:489
  3.8 0.0 copy-start.9
  3.8 1.3 %reshape.20.w0 = bf16[2,384,384]{2,1,0:T(8,128)(2,1)} reshape(bf16[768,3,128]{2,1,0:T(4,128)(2,1)S(1)} %copy.25) | data formatting | bytes 1179648 | tf_op jit(solution)/shard_map/reshape | solution.py:489
  5.1 0.0 copy-done.9
  5.1 0.5 copy.26
  5.6 0.0 copy-start
  5.6 0.0 copy-start.1
  5.6 0.0 copy-start.2
  5.6 0.0 copy-start.3
  5.6 0.0 copy-start.4
  5.6 0.0 copy-start.5
  5.6 0.0 copy-start.6
  5.7 0.0 copy-start.7
  5.7 0.0 copy-start.8
  5.7 1.3 %reshape.21.w1 = bf16[2,384,384]{2,1,0:T(8,128)(2,1)} reshape(bf16[768,3,128]{2,1,0:T(4,128)(2,1)S(1)} %copy.26) | data formatting | bytes 1179648 | tf_op jit(solution)/shard_map/reshape | solution.py:489
  6.9 0.0 copy-done
  6.9 0.0 copy-done.1
  6.9 0.0 copy-done.2
  7.0 0.0 copy-done.3
  7.0 0.0 copy-done.4
  7.0 0.0 copy-done.5
  7.0 0.0 copy-done.6
  7.0 0.0 copy-done.7
  7.0 0.0 copy-done.8
  7.0 96.8 %shard_map.176 = (bf16[256,768]{1,0:T(8,128)(2,1)S(1)}, bf16[256,768]{1,0:T(8,128)(2,1)S(1)}) custom-call(s32[1]{0:T(128)S(6)} %copy.31.text_len, s32[16]{0:T(128)S(1)} %copy-done.7, s32[16]{0:T(128)S(1)} %copy-done.8, bf16[256,768]{1,0:T(8,128)(2,1)S(1)} %copy-done, bf16[256,768]{1,0:T(8,128)(2,1)} %hid1.1, bf16[2,384,384]{2,1,0:T(8,128)(2,1)} %reshape.20.w0, ...), custom_call_target="tpu_custom_call" | custom-call | tf_op jit(solution)/shard_map/pallas_call | solution.py:503
  103.8 0.7 copy.32
  104.6 0.7 copy.33
Async XLA Ops:
  0.6 1.5 %copy-start.10 = (f32[3,3072]{1,0:T(4,128)S(1)}, f32[3,3072]{1,0:T(4,128)}, u32[]{:S(2)}) copy-start(f32[3,3072]{1,0:T(4,128)} %param.24) | copy-start | bytes 110596
  3.8 1.3 %copy-start.9 = (bf16[768,3,128]{2,0,1:T(8,128)(2,1)S(1)}, bf16[768,3,128]{2,0,1:T(8,128)(2,1)}, u32[]{:S(2)}) copy-start(bf16[768,3,128]{2,0,1:T(8,128)(2,1)} %param.20) | copy-start | bytes 1769476
  5.6 1.4 %copy-start = (bf16[256,768]{1,0:T(8,128)(2,1)S(1)}, bf16[256,768]{1,0:T(8,128)(2,1)}, u32[]{:S(2)}) copy-start(bf16[256,768]{1,0:T(8,128)(2,1)} %hid0.1) | copy-start | bytes 1179652
  5.6 1.4 %copy-start.1 = (bf16[2,256,128]{2,1,0:T(8,128)(2,1)S(1)}, bf16[2,256,128]{2,1,0:T(8,128)(2,1)}, u32[]{:S(2)}) copy-start(bf16[2,256,128]{2,1,0:T(8,128)(2,1)} %stale0.1) | copy-start | bytes 393220
  5.6 1.3 %copy-start.2 = (bf16[2,256,128]{2,1,0:T(8,128)(2,1)S(1)}, bf16[2,256,128]{2,1,0:T(8,128)(2,1)}, u32[]{:S(2)}) copy-start(bf16[2,256,128]{2,1,0:T(8,128)(2,1)} %stale1.1) | copy-start | bytes 393220
  5.6 1.3 %copy-start.3 = (bf16[2,256,128]{2,1,0:T(8,128)(2,1)S(1)}, bf16[2,256,128]{2,1,0:T(8,128)(2,1)}, u32[]{:S(2)}) copy-start(bf16[2,256,128]{2,1,0:T(8,128)(2,1)} %text0.1) | copy-start | bytes 393220
  5.6 1.3 %copy-start.4 = (bf16[2,256,128]{2,1,0:T(8,128)(2,1)S(1)}, bf16[2,256,128]{2,1,0:T(8,128)(2,1)}, u32[]{:S(2)}) copy-start(bf16[2,256,128]{2,1,0:T(8,128)(2,1)} %text1.1) | copy-start | bytes 393220
  5.6 1.3 %copy-start.5 = (f32[2,128]{1,0:T(2,128)S(1)}, f32[2,128]{1,0:T(2,128)}, u32[]{:S(2)}) copy-start(f32[2,128]{1,0:T(2,128)} %gain0.1) | copy-start | bytes 3076
  5.6 1.3 %copy-start.6 = (f32[2,128]{1,0:T(2,128)S(1)}, f32[2,128]{1,0:T(2,128)}, u32[]{:S(2)}) copy-start(f32[2,128]{1,0:T(2,128)} %gain1.1) | copy-start | bytes 3076
  5.7 1.3 %copy-start.7 = (s32[16]{0:T(128)S(1)}, s32[16]{0:T(128)}, u32[]{:S(2)}) copy-start(s32[16]{0:T(128)} %ctrl_order.1) | copy-start | bytes 196
  5.7 1.3 %copy-start.8 = (s32[16]{0:T(128)S(1)}, s32[16]{0:T(128)}, u32[]{:S(2)}) copy-start(s32[16]{0:T(128)} %base_order.1) | copy-start | bytes 196

commit v2 on v1

--- a/solution.py
+++ b/solution.py
@@ -9,6 +9,7 @@
 
 F32 = jnp.float32
 BF16 = jnp.bfloat16
+PARTS = 2
 
 
 def kernel(
@@ -37,6 +38,7 @@
     kvbuf,
     psend,
     pbuf,
+    pair,
     hn,
     score_buf,
     blk_send,
@@ -52,6 +54,8 @@
     kv_recv,
     p_send,
     p_recv,
+    pair_send,
+    pair_recv,
     b_send,
     b_recv,
 ):
@@ -128,7 +132,7 @@
 
     def w_copy(b, t, side):
         j = z - t if side == 0 else z + t
-        src = ws[b].at[g] if t == 0 else wbuf.at[b, j, g]
+        src = ws[b].at[:, g] if t == 0 else wbuf.at[b, j, g]
         dev = device(z_=z + 1 if side == 0 else z - 1)
         return remote(src, wbuf.at[b, j, g], w_send.at[b, side, t], w_recv.at[b, j], dev)
 
@@ -209,10 +213,13 @@
                 device(g_=1 - g),
             ).wait_recv()
 
+    def mod_row(b, i, s):
+        if len(mods[b].shape) == 3:
+            return mods[b][i * n_sh + s]
+        return mods[b][i : i + 1, pl.ds(pl.multiple_of(s * cols, cols), cols)]
+
     def normalize(b):
         step = min(32, rows)
-        mod = mods[b]
-
         def body(i, carry):
             at = pl.ds(pl.multiple_of(i * step, step), step)
             total = jnp.zeros((step, 1), F32)
@@ -226,7 +233,7 @@
             inv = lax.rsqrt(spread * (1.0 / width) + 1e-06)
             for s in range(n_sh):
                 normed = (hbuf[b, s, at, :].astype(F32) - center) * inv
-                hn[s, at, :] = (normed * (1.0 + mod[n_sh + s]) + mod[s]).astype(BF16)
+                hn[s, at, :] = (normed * (1.0 + mod_row(b, 1, s)) + mod_row(b, 0, s)).astype(BF16)
             return carry
 
         lax.fori_loop(0, rows // step, body, 0)
@@ -236,18 +243,20 @@
         return (values * lax.rsqrt(mean + 1e-06) * gain).astype(BF16)
 
     def project(b):
-        half = ws[b].shape[1]
+        half = ws[b].shape[2]
 
         def body(s, acc):
             for part in range(2):
                 acc += jnp.dot(
                     hn[s, :, part * half : (part + 1) * half],
-                    wbuf[b, s, part],
+                    jnp.concatenate([wbuf[b, s, part, i] for i in range(3)], axis=1),
                     preferred_element_type=F32,
                 )
             return acc
 
-        qkv = lax.fori_loop(0, n_sh, body, jnp.zeros((rows, 3 * head_size), F32))
+        qkv = lax.fori_loop(
+            0, n_sh, body, jnp.zeros((rows, 3 * head_size), F32), unroll=n_sh <= 4
+        )
         gain = gains[b]
         query = rms(qkv[:, :head_size], gain[0:1, :])
         kvbuf[b, z, 0] = rms(qkv[:, head_size : 2 * head_size], gain[1:2, :])
@@ -266,7 +275,7 @@
 
         slots = text.shape[1]
         text_score = scores(text[0])
-        spot = lax.broadcasted_iota(jnp.int32, (rows, slots), 1)
+        spot = lax.broadcasted_iota(jnp.int32, (query.shape[0], slots), 1)
         text_score = jnp.where(spot < text_len[0], text_score, -1e30)
         top = jnp.max(text_score, axis=1, keepdims=True)
 
@@ -275,7 +284,7 @@
             score_buf[s] = score
             return jnp.maximum(top, jnp.max(score, axis=1, keepdims=True))
 
-        top = lax.fori_loop(0, n_patch, first, top)
+        top = lax.fori_loop(0, n_patch, first, top, unroll=n_patch <= 4)
         expo = jnp.exp(text_score - top)
         total = jnp.sum(expo, axis=1, keepdims=True)
         mixed = jnp.dot(expo.astype(BF16), text[1], preferred_element_type=F32)
@@ -288,23 +297,30 @@
                 mixed + jnp.dot(expo.astype(BF16), kvbuf[b, s, 1], preferred_element_type=F32),
             )
 
-        total, mixed = lax.fori_loop(0, n_patch, second, (total, mixed))
+        total, mixed = lax.fori_loop(
+            0, n_patch, second, (total, mixed), unroll=n_patch <= 4
+        )
         return (mixed / total).astype(BF16)
 
-    def p_copy(b, k):
-        s = peer(k)
-        return remote(
-            psend.at[b, s],
-            pbuf.at[b, me],
-            p_send.at[b, s],
-            p_recv.at[b, me],
-            device(x_=s // n_head, c_=lax.rem(s, n_head)),
-        )
-
-    def peer(k):
-        if k < n_sh - n_head:
-            return lax.rem(x + 1 + k // n_head, n_sec) * n_head + lax.rem(c + k, n_head)
-        return x * n_head + (other if k == n_sh - n_head else c)
+    piece = rows // PARTS
+
+    def rows_of(r):
+        return pl.ds(r * piece, piece)
+
+    def section_of(k):
+        return lax.rem(x + 1 + k, n_sec)
+
+    def pair_copy(b, r, k):
+        o = section_of(k)
+        src = psend.at[b, o * n_head + other, rows_of(r)]
+        dst = pair.at[b, o, rows_of(r)]
+        return remote(src, dst, pair_send.at[b, r, o], pair_recv.at[b, r, o], device(c_=other))
+
+    def p_copy(b, r, k):
+        o = section_of(k)
+        src = psend.at[b, o * n_head + c, rows_of(r)]
+        dst = pbuf.at[b, x, rows_of(r)]
+        return remote(src, dst, p_send.at[b, r, o], p_recv.at[b, r, x], device(x_=o))
 
     def out_part(b, attn, s):
         wo = wos[b]
@@ -314,28 +330,46 @@
             weight = wo[:, pl.ds(pl.multiple_of(s * cols, cols), cols)]
         return jnp.dot(attn, weight, preferred_element_type=F32).astype(BF16)
 
-    def out_start(b, attn):
-        for k in range(n_sh - 1):
-            s = peer(k)
-            psend[b, s] = out_part(b, attn, s)
-            p_copy(b, k).start()
-        pbuf[b, me] = out_part(b, attn, me)
-
-    def out_wait(b):
-        for k in range(n_sh - 1):
-            s = peer(k)
+    def out_start(b, r, attn):
+        for k in range(n_sec):
+            s = section_of(k) * n_head + other
+            psend[b, s, rows_of(r), :] = out_part(b, attn, s)
+            pair_copy(b, r, k).start()
+        for k in range(n_sec - 1):
+            o = section_of(k)
+            mine = out_part(b, attn, o * n_head + c).astype(F32)
+            pair_copy(b, r, k).wait_recv()
+            total = mine + pair[b, o, rows_of(r), :].astype(F32)
+            psend[b, o * n_head + c, rows_of(r), :] = total.astype(BF16)
+            p_copy(b, r, k).start()
+        pbuf[b, x, rows_of(r), :] = out_part(b, attn, me)
+
+    def out_wait(b, r):
+        pair_copy(b, r, n_sec - 1).wait_recv()
+        for k in range(n_sec - 1):
+            o = section_of(k)
             remote(
-                psend.at[b, s], pbuf.at[b, s], p_send.at[b, s], p_recv.at[b, s], device(c_=other)
+                pbuf.at[b, o, rows_of(r)],
+                pbuf.at[b, o, rows_of(r)],
+                p_send.at[b, r, o],
+                p_recv.at[b, r, o],
+                device(c_=other),
             ).wait_recv()
 
+    def attend_out(b, query):
+        for r in range(PARTS):
+            out_start(b, r, attend(b, query[r * piece : (r + 1) * piece]))
+
     def gated(b, at):
-        total = pbuf[b, 0, at, :].astype(F32)
-        for s in range(1, n_sh):
-            total += pbuf[b, s, at, :].astype(F32)
-        return hids[b][at, :].astype(F32) + mods[b][2 * n_sh + me] * total
+        total = pair[b, x, at, :].astype(F32)
+        for o in range(n_sec):
+            total += pbuf[b, o, at, :].astype(F32)
+        return hids[b][at, :].astype(F32) + mod_row(b, 2, me) * total
 
     def ctrl_finish():
         for d in range(n_patch):
+            if d * PARTS % n_patch == 0:
+                out_wait(0, d * PARTS // n_patch)
             at = pl.ds(d * blk, blk)
             out0[at, :] = gated(0, at).astype(BF16)
 
@@ -383,14 +417,15 @@
                 return block + found * blk_buf[s].astype(F32)
 
             relaid = lax.fori_loop(0, n_patch, outer, jnp.zeros((blk, cols), F32))
+            if i * PARTS % n_patch == 0:
+                out_wait(1, i * PARTS // n_patch)
             out1[at, :] = (gated(1, at) + relaid).astype(BF16)
 
     barrier = pltpu.get_barrier_semaphore()
     partners = [device(g_=1 - g)]
     partners += [device(z_=lax.rem(z + k, n_patch)) for k in range(1, n_patch)]
-    for k in range(n_sh - 1):
-        s = peer(k)
-        partners.append(device(x_=s // n_head, c_=lax.rem(s, n_head)))
+    partners += [device(x_=section_of(k)) for k in range(n_sec - 1)]
+    partners.append(device(c_=other))
     for partner in partners:
         pl.semaphore_signal(
             barrier, inc=1, device_id=partner, device_id_type=pl.DeviceIdType.MESH
@@ -401,41 +436,41 @@
     chain_start(w_copy, 0, 0)
     hid_start(0)
     chain_start(kv_copy, 0, 0)
-    wbuf[0, z] = ws[0][...]
-    wbuf[1, z] = ws[1][...]
+    for b in range(2):
+        for part in range(2):
+            wbuf[b, z, part] = ws[b][:, part]
     hid_start(1)
     hid_forward(0)
     w_arrive(0, 0)
     kv_arrive(0, 0)
     chain_start(w_copy, 1, 0)
-    for t in range(1, last):
+    hid_wait(0)
+    normalize(0)
+    for t in range(1, last - 1):
         w_arrive(0, t)
         kv_arrive(0, t)
-        if t == 1:
-            hid_wait(0)
-            normalize(0)
-            hid_forward(1)
-            chain_start(kv_copy, 1, 0)
+    hid_forward(1)
     w_arrive(1, 0)
+    w_arrive(0, last - 1)
     w_wait(0)
     query = project(0)
-    kv_arrive(1, 0)
+    chain_start(kv_copy, 1, 0)
     for t in range(1, last - 1):
         w_arrive(1, t)
+    kv_arrive(0, last - 1)
+    attend_out(0, query)
+    for t in range(last - 1):
         kv_arrive(1, t)
-    out_start(0, attend(0, query))
-    w_arrive(1, last - 1)
-    kv_arrive(1, last - 1)
     hid_wait(1)
     normalize(1)
-    out_wait(0)
+    w_arrive(1, last - 1)
     ctrl_finish()
     relay_start()
     w_wait(1)
     query = project(1)
-    out_start(1, attend(1, query))
+    kv_arrive(1, last - 1)
+    attend_out(1, query)
     relay_wait()
-    out_wait(1)
     base_finish()
 
     for b in range(2):
@@ -453,8 +488,12 @@
 
         for k in range(1, n_patch):
             y_copy(b, lax.rem(z + k, n_patch)).wait_send()
-        for k in range(n_sh - 1):
-            p_copy(b, k).wait_send()
+        for k in range(n_sec - 1):
+            for r in range(PARTS):
+                p_copy(b, r, k).wait_send()
+        for k in range(n_sec):
+            for r in range(PARTS):
+                pair_copy(b, r, k).wait_send()
     for k in range(1, n_patch):
         b_copy(k).wait_send()
 
@@ -486,7 +525,7 @@
     blk = rows // n_patch
 
     def halves(weight):
-        return weight.reshape(2, w_rows // 2, 3 * head_size)
+        return weight.transpose(1, 0, 2).reshape(3, 2, w_rows // 2, head_size)
 
     def by_columns(weight):
         if cols % 128 == 0:
@@ -494,7 +533,7 @@
         return weight.reshape(weight.shape[0], n_sh, cols).transpose(1, 0, 2)
 
     def mod_rows(mod):
-        return mod.reshape(3 * n_sh, 1, cols)
+        return mod if cols % 128 == 0 else mod.reshape(3 * n_sh, 1, cols)
 
     smem = pl.BlockSpec(memory_space=pltpu.SMEM)
     vmem = pl.BlockSpec(memory_space=pltpu.VMEM)
@@ -507,12 +546,13 @@
         out_specs=(vmem, vmem),
         scratch_shapes=[
             pltpu.VMEM((2, n_sh, rows, cols), BF16),
-            pltpu.VMEM((2, n_patch, 2, w_rows // 2, 3 * head_size), BF16),
+            pltpu.VMEM((2, n_patch, 2, 3, w_rows // 2, head_size), BF16),
             pltpu.VMEM((2, n_patch, 2, rows, head_size), BF16),
             pltpu.VMEM((2, n_sh, rows, cols), BF16),
-            pltpu.VMEM((2, n_sh, rows, cols), BF16),
+            pltpu.VMEM((2, n_sec, rows, cols), BF16),
+            pltpu.VMEM((2, n_sec, rows, cols), BF16),
             pltpu.VMEM((n_sh, rows, cols), BF16),
-            pltpu.VMEM((n_patch, rows, rows), F32),
+            pltpu.VMEM((n_patch, rows // PARTS, rows), F32),
             pltpu.VMEM((n_patch, blk, cols), BF16),
             pltpu.VMEM((n_patch, blk, cols), BF16),
             dma((2, n_sec)),
@@ -524,8 +564,10 @@
             dma((2, n_patch)),
             dma((2, 2, n_patch)),
             dma((2, n_patch)),
-            dma((2, n_sh)),
-            dma((2, n_sh)),
+            dma((2, PARTS, n_sec)),
+            dma((2, PARTS, n_sec)),
+            dma((2, PARTS, n_sec)),
+            dma((2, PARTS, n_sec)),
             dma((n_patch,)),
             dma((n_patch,)),
         ],

time: 106 us -> 98.4 us (0.928)
  Pallas kernels: 96.8 us -> 88.3 us
  local copies, waits for them, and re-layouts: 7.06 us -> 8.38 us
    pallas_call x1, Pallas kernels: 96.8 us -> 88.3 us  [local(): pl.pallas_call(functools.partial(kernel, sizes), out_shape=(out, out), in...]
    unnamed x24, local copies, waits for them, and re-layouts: 1.56 us -> 8.38 us
    reshape x6 -> x0, local copies, waits for them, and re-layouts: 5.5 us -> none  [the longest x4 4.59 us: halves(): return weight.reshape(2, w_rows // 2, 3 * head_size)]
where the time goes in v2:
time: 98.4 us; the launch traced here: 98 us
  Pallas kernels  88.3 us (90%)
  local copies, waits for them, and re-layouts  8.38 us (9%)
  between operations  1.33 us (1%)
    pallas_call x1, Pallas kernels, local(): pl.pallas_call(functools.partial(kernel, sizes), out_shape=(out, out), in...  88.3 us
    unnamed x24, local copies, waits for them, and re-layouts  8.38 us

profile of v2, /device:TPU:0, one launch (start us, length us, event | category | flops | bytes accessed | tf_op | source)
XLA Modules:
  0.0 98.0 jit_solution(4632410541410198089)
XLA Ops:
  1.3 0.0 copy-start.8
  1.3 0.0 copy-start.10
  1.3 0.0 copy-start.7
  1.3 0.0 copy-start.9
  1.3 0.6 copy-done.8
  2.0 0.0 copy-done.10
  2.0 0.0 copy-done.7
  2.0 0.0 copy-done.9
  2.0 0.0 copy-start
  2.0 1.0 %copy-done = bf16[256,768]{1,0:T(8,128)(2,1)S(1)} copy-done((bf16[256,768]{1,0:T(8,128)(2,1)S(1)}, bf16[256,768]{1,0:T(8,128)(2,1)}, u32[]{:S(2)}) %copy-start) | copy-done | bytes 393240
  3.0 0.0 copy-start.1
  3.0 0.9 copy-done.1
  3.9 0.0 copy-start.2
  3.9 0.9 copy-done.2
  4.8 0.0 copy-start.3
  4.8 0.9 copy-done.3
  5.7 0.0 copy-start.4
  5.7 0.9 copy-done.4
  6.6 0.0 copy-start.5
  6.6 0.8 copy-done.5
  7.4 0.0 copy-start.6
  7.4 0.8 copy-done.6
  8.2 88.3 %shard_map.176 = (bf16[256,768]{1,0:T(8,128)(2,1)S(1)}, bf16[256,768]{1,0:T(8,128)(2,1)S(1)}) custom-call(s32[1]{0:T(128)S(6)} %copy.21.text_len, s32[16]{0:T(128)S(1)} %copy-done.9, s32[16]{0:T(128)S(1)} %copy-done.10, bf16[256,768]{1,0:T(8,128)(2,1)S(1)} %copy-done, bf16[256,768]{1,0:T(8,128)(2,1)} %hid1.1, bf16[3,2,384,128]{3,2,1,0:T(8,128)(2,1)} %bitcast.6, ...), custom_call_target="tpu_custom_call" | custom-call | tf_op jit(solution)/shard_map/pallas_call | solution.py:542
  96.5 0.7 copy.22
  97.3 0.7 copy.23
Async XLA Ops:
  1.3 0.7 copy-start.8
  1.3 0.7 copy-start.10
  1.3 0.7 copy-start.7
  1.3 0.7 copy-start.9
  2.0 1.0 %copy-start = (bf16[256,768]{1,0:T(8,128)(2,1)S(1)}, bf16[256,768]{1,0:T(8,128)(2,1)}, u32[]{:S(2)}) copy-start(bf16[256,768]{1,0:T(8,128)(2,1)} %hid0.1) | copy-start | bytes 1179652
  3.0 0.9 copy-start.1
  3.9 0.9 copy-start.2
  4.8 0.9 copy-start.3
  5.7 0.9 copy-start.4
  6.6 0.8 copy-start.5
  7.4 0.8 copy-start.6

commit v3 on v2

--- a/solution.py
+++ b/solution.py
@@ -58,9 +58,20 @@
     pair_recv,
     b_send,
     b_recv,
+    load_sem,
+    *held,
 ):
     n_groups, n_patch, n_sec, n_head = sizes
     n_sh = n_sec * n_head
+    sources = (hid0, hid1, w0, w1, wo0, wo1, mod0, mod1, gain0, gain1, text0, text1)
+    src_hids, src_ws = (hid0, hid1), (w0, w1)
+    loads = [
+        pltpu.make_async_copy(src, dst, load_sem.at[i])
+        for i, (src, dst) in enumerate(zip(sources, held))
+    ]
+    for load in loads:
+        load.start()
+    hid0, hid1, w0, w1, wo0, wo1, mod0, mod1, gain0, gain1, text0, text1 = held
     hids, ws, wos = (hid0, hid1), (w0, w1), (wo0, wo1)
     mods, gains, stales, texts, outs = (
         (mod0, mod1),
@@ -99,7 +110,7 @@
         )
 
     def hid_copy(b, k):
-        src = hids[b]
+        src = src_hids[b]
         if k == 0:
             dev = device(c_=other)
         else:
@@ -109,7 +120,6 @@
     def hid_start(b):
         for k in list(range(1, n_sec)) + [0]:
             hid_copy(b, k).start()
-        hbuf[b, me] = hids[b][...]
 
     def hid_fwd_copy(b, k):
         j = lax.rem(x + n_sec - k, n_sec) * n_head + c
@@ -132,7 +142,7 @@
 
     def w_copy(b, t, side):
         j = z - t if side == 0 else z + t
-        src = ws[b].at[:, g] if t == 0 else wbuf.at[b, j, g]
+        src = src_ws[b].at[:, g] if t == 0 else wbuf.at[b, j, g]
         dev = device(z_=z + 1 if side == 0 else z - 1)
         return remote(src, wbuf.at[b, j, g], w_send.at[b, side, t], w_recv.at[b, j], dev)
 
@@ -436,10 +446,13 @@
     chain_start(w_copy, 0, 0)
     hid_start(0)
     chain_start(kv_copy, 0, 0)
+    hid_start(1)
+    for load in loads:
+        load.wait()
     for b in range(2):
+        hbuf[b, me] = hids[b][...]
         for part in range(2):
             wbuf[b, z, part] = ws[b][:, part]
-    hid_start(1)
     hid_forward(0)
     w_arrive(0, 0)
     kv_arrive(0, 0)
@@ -535,14 +548,32 @@
     def mod_rows(mod):
         return mod if cols % 128 == 0 else mod.reshape(3 * n_sh, 1, cols)
 
+    operands = (
+        ctrl_hidden,
+        base_hidden,
+        halves(ctrl_qkv_weight),
+        halves(base_qkv_weight),
+        by_columns(ctrl_out_weight),
+        by_columns(base_out_weight),
+        mod_rows(ctrl_mod),
+        mod_rows(base_mod),
+        ctrl_qk_gain,
+        base_qk_gain,
+        ctrl_stale,
+        base_stale,
+        ctrl_text,
+        base_text,
+    )
+    held = operands[:10] + operands[12:]
     smem = pl.BlockSpec(memory_space=pltpu.SMEM)
     vmem = pl.BlockSpec(memory_space=pltpu.VMEM)
+    hbm = pl.BlockSpec(memory_space=pltpu.HBM)
     dma = pltpu.SemaphoreType.DMA
     out = jax.ShapeDtypeStruct((rows, cols), BF16)
     return pl.pallas_call(
         functools.partial(kernel, sizes),
         out_shape=(out, out),
-        in_specs=[smem] * 3 + [vmem] * 14,
+        in_specs=[smem] * 3 + [hbm] * 14,
         out_specs=(vmem, vmem),
         scratch_shapes=[
             pltpu.VMEM((2, n_sh, rows, cols), BF16),
@@ -570,28 +601,17 @@
             dma((2, PARTS, n_sec)),
             dma((n_patch,)),
             dma((n_patch,)),
-        ],
+            dma((len(held),)),
+        ]
+        + [pltpu.VMEM(array.shape, array.dtype) for array in held],
         compiler_params=pltpu.CompilerParams(
-            collective_id=0, has_side_effects=True, vmem_limit_bytes=52 * 1024 * 1024
+            collective_id=0, has_side_effects=True, vmem_limit_bytes=56 * 1024 * 1024
         ),
     )(
         text_len,
         ctrl_order,
         base_order,
-        ctrl_hidden,
-        base_hidden,
-        halves(ctrl_qkv_weight),
-        halves(base_qkv_weight),
-        by_columns(ctrl_out_weight),
-        by_columns(base_out_weight),
-        mod_rows(ctrl_mod),
-        mod_rows(base_mod),
-        ctrl_qk_gain,
-        base_qk_gain,
-        ctrl_stale,
-        base_stale,
-        ctrl_text,
-        base_text,
+        *operands,
     )
 
 

time: 98.4 us -> 92.4 us (0.939)
  local copies, waits for them, and re-layouts: 8.38 us -> 2.57 us
    unnamed x24 -> x4, local copies, waits for them, and re-layouts: 8.38 us -> 2.57 us
where the time goes in v3:
time: 92.4 us; the launch traced here: 92.2 us
  Pallas kernels  88.4 us (96%)
  local copies, waits for them, and re-layouts  2.57 us (3%)
  between operations  1.3 us (1%)
    pallas_call x1, Pallas kernels, local(): pl.pallas_call(functools.partial(kernel, sizes), out_shape=(out, out), in...  88.4 us
    unnamed x4, local copies, waits for them, and re-layouts  2.57 us

profile of v3, /device:TPU:0, one launch (start us, length us, event | category | flops | bytes accessed | tf_op | source)
XLA Modules:
  0.0 92.2 jit_solution(6699116251480042025)
XLA Ops:
  1.3 88.4 %shard_map.176 = (bf16[256,768]{1,0:T(8,128)(2,1)}, bf16[256,768]{1,0:T(8,128)(2,1)}) custom-call(s32[1]{0:T(128)S(6)} %copy.21.text_len, s32[16]{0:T(128)} %ctrl_order.1, s32[16]{0:T(128)} %base_order.1, bf16[256,768]{1,0:T(8,128)(2,1)} %hid0.1, bf16[256,768]{1,0:T(8,128)(2,1)} %hid1.1, bf16[3,2,384,128]{3,2,1,0:T(8,128)(2,1)} %bitcast.6, ...), custom_call_target="tpu_custom_call" | custom-call | tf_op jit(solution)/shard_map/pallas_call | solution.py:573
  89.7 0.0 copy-start
  89.7 1.8 %copy.22 = bf16[256,768]{1,0:T(8,128)(2,1)} copy(bf16[256,768]{1,0:T(8,128)(2,1)} %get-tuple-element.4) | data formatting | bytes 786432
  91.5 0.0 copy-done
  91.5 0.7 copy.23
Async XLA Ops:
  89.7 1.8 %copy-start = (bf16[256,768]{1,0:T(8,128)(2,1)S(1)}, bf16[256,768]{1,0:T(8,128)(2,1)}, u32[]{:S(2)}) copy-start(bf16[256,768]{1,0:T(8,128)(2,1)} %get-tuple-element.5) | copy-start | bytes 1179652

commit v4 on v3

--- a/solution.py
+++ b/solution.py
@@ -446,6 +446,7 @@
     chain_start(w_copy, 0, 0)
     hid_start(0)
     chain_start(kv_copy, 0, 0)
+    chain_start(w_copy, 1, 0)
     hid_start(1)
     for load in loads:
         load.wait()
@@ -456,14 +457,13 @@
     hid_forward(0)
     w_arrive(0, 0)
     kv_arrive(0, 0)
-    chain_start(w_copy, 1, 0)
-    hid_wait(0)
-    normalize(0)
     for t in range(1, last - 1):
         w_arrive(0, t)
         kv_arrive(0, t)
     hid_forward(1)
     w_arrive(1, 0)
+    hid_wait(0)
+    normalize(0)
     w_arrive(0, last - 1)
     w_wait(0)
     query = project(0)

time: 92.4 us -> 90 us (0.974)
  Pallas kernels: 88.4 us -> 86 us
    pallas_call x1, Pallas kernels: 88.4 us -> 86 us  [local(): pl.pallas_call(functools.partial(kernel, sizes), out_shape=(out, out), in...]
where the time goes in v4:
time: 90 us; the launch traced here: 89.9 us
  Pallas kernels  86 us (96%)
  local copies, waits for them, and re-layouts  2.57 us (3%)
  between operations  1.3 us (1%)
    pallas_call x1, Pallas kernels, local(): pl.pallas_call(functools.partial(kernel, sizes), out_shape=(out, out), in...  86 us
    unnamed x4, local copies, waits for them, and re-layouts  2.57 us

profile of v4, /device:TPU:0, one launch (start us, length us, event | category | flops | bytes accessed | tf_op | source)
XLA Modules:
  0.0 89.9 jit_solution(13712492284314981902)
XLA Ops:
  1.3 86.0 %shard_map.176 = (bf16[256,768]{1,0:T(8,128)(2,1)}, bf16[256,768]{1,0:T(8,128)(2,1)}) custom-call(s32[1]{0:T(128)S(6)} %copy.21.text_len, s32[16]{0:T(128)} %ctrl_order.1, s32[16]{0:T(128)} %base_order.1, bf16[256,768]{1,0:T(8,128)(2,1)} %hid0.1, bf16[256,768]{1,0:T(8,128)(2,1)} %hid1.1, bf16[3,2,384,128]{3,2,1,0:T(8,128)(2,1)} %bitcast.6, ...), custom_call_target="tpu_custom_call" | custom-call | tf_op jit(solution)/shard_map/pallas_call | solution.py:573
  87.3 0.0 copy-start
  87.3 1.8 %copy.22 = bf16[256,768]{1,0:T(8,128)(2,1)} copy(bf16[256,768]{1,0:T(8,128)(2,1)} %get-tuple-element.4) | data formatting | bytes 786432
  89.1 0.0 copy-done
  89.1 0.7 copy.23
Async XLA Ops:
  87.3 1.8 %copy-start = (bf16[256,768]{1,0:T(8,128)(2,1)S(1)}, bf16[256,768]{1,0:T(8,128)(2,1)}, u32[]{:S(2)}) copy-start(bf16[256,768]{1,0:T(8,128)(2,1)} %get-tuple-element.5) | copy-start | bytes 1179652

commit v5 on v4

--- a/solution.py
+++ b/solution.py
@@ -462,12 +462,12 @@
         kv_arrive(0, t)
     hid_forward(1)
     w_arrive(1, 0)
+    chain_start(kv_copy, 1, 0)
     hid_wait(0)
     normalize(0)
     w_arrive(0, last - 1)
     w_wait(0)
     query = project(0)
-    chain_start(kv_copy, 1, 0)
     for t in range(1, last - 1):
         w_arrive(1, t)
     kv_arrive(0, last - 1)

time: 90 us -> 91.4 us (1.016)
  Pallas kernels: 86 us -> 87.4 us
    pallas_call x1, Pallas kernels: 86 us -> 87.4 us  [local(): pl.pallas_call(functools.partial(kernel, sizes), out_shape=(out, out), in...]
where the time goes in v5:
time: 91.4 us; the launch traced here: 91.2 us
  Pallas kernels  87.4 us (96%)
  local copies, waits for them, and re-layouts  2.57 us (3%)
  between operations  1.3 us (1%)
    pallas_call x1, Pallas kernels, local(): pl.pallas_call(functools.partial(kernel, sizes), out_shape=(out, out), in...  87.4 us
    unnamed x4, local copies, waits for them, and re-layouts  2.57 us

profile of v5, /device:TPU:0, one launch (start us, length us, event | category | flops | bytes accessed | tf_op | source)
XLA Modules:
  0.0 91.2 jit_solution(15638224644791695277)
XLA Ops:
  1.3 87.4 %shard_map.176 = (bf16[256,768]{1,0:T(8,128)(2,1)}, bf16[256,768]{1,0:T(8,128)(2,1)}) custom-call(s32[1]{0:T(128)S(6)} %copy.21.text_len, s32[16]{0:T(128)} %ctrl_order.1, s32[16]{0:T(128)} %base_order.1, bf16[256,768]{1,0:T(8,128)(2,1)} %hid0.1, bf16[256,768]{1,0:T(8,128)(2,1)} %hid1.1, bf16[3,2,384,128]{3,2,1,0:T(8,128)(2,1)} %bitcast.6, ...), custom_call_target="tpu_custom_call" | custom-call | tf_op jit(solution)/shard_map/pallas_call | solution.py:573
  88.7 0.0 copy-start
  88.7 1.8 %copy.22 = bf16[256,768]{1,0:T(8,128)(2,1)} copy(bf16[256,768]{1,0:T(8,128)(2,1)} %get-tuple-element.4) | data formatting | bytes 786432
  90.5 0.0 copy-done
  90.5 0.7 copy.23
Async XLA Ops:
  88.7 1.8 %copy-start = (bf16[256,768]{1,0:T(8,128)(2,1)S(1)}, bf16[256,768]{1,0:T(8,128)(2,1)}, u32[]{:S(2)}) copy-start(bf16[256,768]{1,0:T(8,128)(2,1)} %get-tuple-element.5) | copy-start | bytes 1179652
